TPU v7x, 32 devices: a whole 2x2x4 slice. The times are simulated.
32 devices in a mesh: dom: 8 (over z, y), rep: 4 (over x, core).
Axes of the slice: x: 2, y: 2, z: 4, core: 2. Of those that a mesh axis runs over, the one named last changes fastest.
Arguments:
- x_loader: bfloat16 [16384, 512], P(('dom', 'rep')), may hold values from -6 to 6
- owner_index: int32 [16384], P(('dom', 'rep')), may hold values from 0 to 16383, as said below
- tile_vals: bfloat16 [128, 12, 128, 128], P(('dom', 'rep')), as said below
- tile_cols: int32 [128, 12], P(('dom', 'rep')), may hold values from 0 to 127, as said below
- tile_live: int32 [128, 12], P(('dom', 'rep')), may hold values from 0 to 1, as said below
- w_self: bfloat16 [512, 512], replicated, may hold values from -0.25 to 0.25
- w_neigh: bfloat16 [512, 512], replicated, may hold values from -3 to 3
- bias: float32 [512], replicated, may hold values from -3 to 3
- cotangent: bfloat16 [16384, 512], P(('dom', 'rep')), may hold values from -6 to 6
Outputs:
- layer_out: bfloat16 [16384, 512], P(('dom', 'rep'))
- grad_features: bfloat16 [16384, 512], P(('dom', 'rep'))
- grad_self: float32 [512, 512], replicated
- grad_neigh: float32 [512, 512], replicated
- grad_bias: float32 [512], replicated
Inputs may be any that keep to these rules, and one draw needn't show every extreme that they name: `owner_index`: A permutation of the 16384 rows. Loader rows are in blocks of 512 in the order of the devices (dom slowest); owner rows likewise. The 512 rows of each loader block with rep index r go to owner blocks of rep index r, 64 rows to each of the 8 partitions. `tile_cols`: partition p holds row tiles p * 16 to (p + 1) * 16 - 1. A column tile of a row tile of partition p lies in partition p or within 4 tiles beyond its edges. W is symmetric: every live slot (t, c) with tiles B is matched by a live slot (c, t) with tiles B^T, a slot with c = t holding a symmetric tile. `tile_live`: live slots are symmetric as stated for tile_cols. `tile_vals`: nonnegative edge weights.
All inputs are finite; a program needn't handle non-finite values.
Results may differ from a plain program's by a relative error of at most 0.0075.
Values may be sent and summed in bfloat16 or wider, within the bound.
A program may use at most 64 MiB of HBM per device.

v0:
```python
import jax
import jax.numpy as jnp
from jax import lax
from jax.sharding import PartitionSpec as P

HALO_T = 4


def shifted(value, axis, steps):
    count = lax.axis_size(axis)
    first, last = (max(0, -steps), min(count, count - steps))
    return lax.ppermute(value, axis, [(source, source + steps) for source in range(first, last)])


def with_halo(block, sides, width):
    for axis, dim in sides:
        count = lax.axis_size(axis)
        forward = [(i, i + 1) for i in range(count - 1)]
        backward = [(target, source) for source, target in forward]
        low = lax.ppermute(
            lax.slice_in_dim(block, block.shape[dim] - width, None, axis=dim), axis, forward
        )
        high = lax.ppermute(lax.slice_in_dim(block, 0, width, axis=dim), axis, backward)
        block = jnp.concatenate([low, block, high], axis=dim)
    return block


def contract_rows(left, right):
    return lax.dot_general(
        left, right, (((0,), (0,)), ((), ())), preferred_element_type=jnp.float32
    )


def contract_cols(left, right):
    return lax.dot_general(
        left, right, (((1,), (1,)), ((), ())), preferred_element_type=jnp.float32
    )


def pass_rim(values, offset):
    return shifted(values.astype(jnp.bfloat16), "dom", offset).astype(values.dtype)


def shards(
    x_loader, owner_index, tile_vals, tile_cols, tile_live, w_self, w_neigh, bias, cotangent
):
    rows, width = x_loader.shape
    reps = lax.axis_size("rep")
    dom_place = lax.axis_index("dom")
    part_rows = rows * reps
    part_tiles = part_rows // 128
    row_tiles = rows // 128
    rim_rows = HALO_T * 128
    dest = owner_index // part_rows
    order = jnp.argsort(dest, stable=True)
    moved, slot = (
        lax.all_to_all(x_loader[order], "dom", split_axis=0, concat_axis=0, tiled=True),
        lax.all_to_all((owner_index % rows)[order], "dom", split_axis=0, concat_axis=0, tiled=True),
    )
    features = jnp.zeros((rows, width), jnp.bfloat16).at[slot].set(moved)
    first_tile = dom_place * part_tiles - HALO_T
    local_cols = tile_cols - first_tile
    masked = tile_vals * tile_live.astype(jnp.bfloat16)[:, :, None, None]
    degree = 1.0 + jnp.sum(masked, axis=(1, 3), dtype=jnp.float32)
    whole = lax.all_gather(features, "rep", axis=0, tiled=True)
    extended = with_halo(whole, (("dom", 0),), rim_rows)
    picked = extended.reshape(-1, 128, width)[local_cols]
    summed = jnp.einsum("tkab,tkbf->taf", masked, picked, preferred_element_type=jnp.float32)
    agg = (summed / degree[:, :, None]).reshape(rows, width).astype(jnp.bfloat16)
    pre = (
        jnp.dot(features, w_self, preferred_element_type=jnp.float32)
        + jnp.dot(agg, w_neigh, preferred_element_type=jnp.float32)
        + bias
    )
    layer_out = jnp.where(pre > 0, pre, jnp.expm1(jnp.minimum(pre, 0.0))).astype(jnp.bfloat16)
    slope = jnp.where(pre > 0, 1.0, jnp.exp(jnp.minimum(pre, 0.0)))
    dz = (cotangent.astype(jnp.float32) * slope).astype(jnp.bfloat16)
    grad_self, grad_neigh, grad_bias = lax.psum(
        (
            contract_rows(features, dz),
            contract_rows(agg, dz),
            jnp.sum(dz, axis=0, dtype=jnp.float32),
        ),
        ("dom", "rep"),
    )
    scaled = (contract_cols(dz, w_neigh) / degree.reshape(rows, 1)).astype(jnp.bfloat16)
    terms = jnp.einsum(
        "tkab,taf->tkbf",
        masked,
        scaled.reshape(row_tiles, 128, width),
        preferred_element_type=jnp.float32,
    )
    span_tiles = part_tiles + 2 * HALO_T
    selector = (
        local_cols.reshape(-1)[None, :] == jnp.arange(span_tiles, dtype=jnp.int32)[:, None]
    ).astype(jnp.float32)
    buffer = jnp.einsum(
        "en,nbf->ebf", selector, terms.reshape(-1, 128, width), precision=lax.Precision.HIGHEST
    )
    buffer = buffer.reshape(span_tiles * 128, width)
    lower = buffer[:rim_rows]
    upper = buffer[rim_rows + part_rows :]
    core = buffer[rim_rows : rim_rows + part_rows]
    core = core.at[:rim_rows].add(pass_rim(upper, 1))
    core = core.at[part_rows - rim_rows :].add(pass_rim(lower, -1))
    back = lax.psum_scatter(core, "rep", scatter_dimension=0, tiled=True)
    grad_features = (contract_cols(dz, w_self) + back).astype(jnp.bfloat16)
    return (layer_out, grad_features, grad_self, grad_neigh, grad_bias)


def solution(mesh):
    return jax.shard_map(
        shards,
        mesh=mesh,
        in_specs=(
            P(("dom", "rep"), None),
            P(("dom", "rep")),
            P(("dom", "rep"), None, None, None),
            P(("dom", "rep"), None),
            P(("dom", "rep"), None),
            P(),
            P(),
            P(),
            P(("dom", "rep"), None),
        ),
        out_specs=(P(("dom", "rep"), None), P(("dom", "rep"), None), P(), P(), P()),
        check_vma=False,
    )
```

profile of v0, /device:TPU:1, one launch (start us, length us, event | category | flops | bytes accessed | tf_op | source)
XLA Modules:
  0.0 358.4 jit_solution(8284953067238762718)
XLA Ops:
  8.0 3.8 %sort.17 = (s32[512]{0:T(512)}, s32[512]{0:T(512)S(1)}) sort(s32[512]{0:T(512)S(1)} %get-tuple-element.44, s32[512]{0:T(512)S(1)} %iota.8), dimensions={0}, to_apply=%region_0.1 | sort | flops 4608 | bytes 8192 | tf_op jit(solution)/shard_map/jit(argsort)/sort | solution.py:55
  11.8 3.5 gather_fusion
  16.0 6.4 %all-to-all-start = ((s32[8,64,1]{1,2,0:T(1,128)}), s32[8,64,1]{1,2,0:T(1,128)S(1)}, u32[]{:S(2)}, u32[]{:S(2)}) async-start(s32[8,64,1]{1,2,0:T(1,128)} %bitcast), calls=%async_computation | async-start | bytes 8192 | tf_op jit(solution)/shard_map/all_to_all | solution.py:58
  22.4 2.6 gather_fusion.1
  25.0 2.6 all-to-all-done
  27.6 3.5 all-to-all-start.1
  32.4 9.6 %all-to-all-done.1 = bf16[8,64,512]{2,1,0:T(8,128)(2,1)S(1)} async-done(((bf16[8,64,512]{2,1,0:T(8,128)(2,1)}), bf16[8,64,512]{2,1,0:T(8,128)(2,1)S(1)}, u32[]{:S(2)}, u32[]{:S(2)}) %all-to-all-start.1) | async-done | bytes 524320 | tf_op jit(solution)/shard_map/all_to_all | solution.py:57
  42.0 3.2 scatter_custom_fusion
  45.8 25.4 %all-gather.2.cloned.1.call-done = bf16[2048,512]{1,0:T(8,128)(2,1)} async-done(((bf16[512,512]{1,0:T(8,128)(2,1)}), bf16[2048,512]{1,0:T(8,128)(2,1)}) %all-gather.2.cloned.1.call-update) | async-done | bytes 2097168 | tf_op jit(solution)/shard_map/all_gather | solution.py:65
  71.2 2.2 fusion.25
  73.4 3.9 %collective-permute-start = (bf16[512,512]{1,0:T(8,128)(2,1)}, bf16[512,512]{1,0:T(8,128)(2,1)}, u32[]{:S(2)}, u32[]{:S(2)}) collective-permute-start(bf16[512,512]{1,0:T(8,128)(2,1)} %get-tuple-element.39), channel_id=1, source_target_pairs={{0,4},{4,8},{8,12},{12,16},{16,20},{20,24},{24,28},{1,5},{5,9},{9,... | collective-permute-start | bytes 1572872 | tf_op jit(solution)/shard_map/ppermute | solution.py:20
  80.1 19.0 %collective-permute-done = bf16[512,512]{1,0:T(8,128)(2,1)} collective-permute-done((bf16[512,512]{1,0:T(8,128)(2,1)}, bf16[512,512]{1,0:T(8,128)(2,1)}, u32[]{:S(2)}, u32[]{:S(2)}) %collective-permute-start) | collective-permute-done | bytes 524320 | tf_op jit(solution)/shard_map/ppermute | solution.py:20
  99.1 3.1 pad_maximum_fusion
  102.2 6.9 %gather_fusion.2 = bf16[48,128,512]{2,1,0:T(8,128)(2,1)} fusion(bf16[24,128,512]{2,1,0:T(8,128)(2,1)} %bitcast.48, s32[1024]{0:T(1024)S(1)} %pad_clamp_fusion), kind=kCustom, calls=%fused_computation.2 | custom fusion | bytes 12583104 | tf_op jit(solution)/shard_map/gather | solution.py:67
  109.1 4.0 %fusion.5 = bf16[4,128,512]{2,1,0:T(8,128)(2,1)S(1)} fusion(bf16[4,12,128,512]{3,2,1,0:T(8,128)(2,1)} %bitcast.49, bf16[4,12,128,128]{3,2,1,0:T(8,128)(2,1)S(1)} %copy-done.3, bf16[4,12]{1,0:T(4,128)(2,1)S(1)} %convert_element_type.45, f32[4,128]{1,0:T(4,128)S(1)} %get-tuple-element.43), kind=kOutput, calls=%fused_computation.16 | convolution fusion | flops 806617088 | bytes 8390752 | tf_op jit(solution)/shard_map/tkab,tkbf->taf/dot_general | solution.py:68
  117.3 12.3 %fusion.26 = (bf16[24,128,512]{2,0,1:T(8,128)(2,1)S(1)}, f32[24,128,512]{2,0,1:T(8,128)S(1)}) fusion(f32[48,128,512]{2,1,0:T(8,128)S(1)} %bitcast.47, s32[48]{0:T(128)S(1)} %eq.17), kind=kOutput, calls=%fused_computation.55 | convolution fusion | flops 907543680 | bytes 22020288 | tf_op jit(solution)/shard_map/en,nbf->ebf/dot_general | solution.py:97
  130.2 4.1 %collective-permute-start.2 = (bf16[512,512]{1,0:T(8,128)(2,1)S(1)}, bf16[512,512]{1,0:T(8,128)(2,1)S(1)}, u32[]{:S(2)}, u32[]{:S(2)}) collective-permute-start(bf16[512,512]{1,0:T(8,128)(2,1)S(1)} %bitcast.53), channel_id=1, source_target_pairs={{0,4},{4,8},{8,12},{12,16},{16,20},{20,24},{24,28},{1,5},{5,9},{9,... | collective-permute-start | bytes 1572872 | tf_op jit(solution)/shard_map/ppermute | solution.py:12
  137.0 4.4 %copy.29 = f32[16,128,512]{2,1,0:T(8,128)} copy(f32[16,128,512]{2,0,1:T(8,128)S(1)} %slice.78) | data formatting | bytes 8388608 | tf_op jit(solution)/shard_map/slice | solution.py:103
  141.8 13.8 %collective-permute-done.2 = bf16[512,512]{1,0:T(8,128)(2,1)S(1)} collective-permute-done((bf16[512,512]{1,0:T(8,128)(2,1)S(1)}, bf16[512,512]{1,0:T(8,128)(2,1)S(1)}, u32[]{:S(2)}, u32[]{:S(2)}) %collective-permute-start.2) | collective-permute-done | bytes 524320 | tf_op jit(solution)/shard_map/ppermute | solution.py:12
  156.8 2.4 fusion.12
  162.2 43.4 %psum.23 = f32[512]{0:T(512)} all-reduce(f32[512]{0:T(512)S(1)} %get-tuple-element.33), channel_id=1, replica_groups=mesh['dom'=8,'rep'=4] {'dom','rep'}, use_global_device_ids=true, to_apply=%region_7.8 | all-reduce | flops 512 | bytes 4096 | tf_op jit(solution)/shard_map/psum | solution.py:78
  209.4 137.9 %all-reduce.3.cloned.1.call-done = (f32[512,512]{1,0:T(8,128)}, f32[512,512]{1,0:T(8,128)}) async-done(((f32[512,512]{1,0:T(8,128)}, f32[512,512]{1,0:T(8,128)}), (f32[512,512]{1,0:T(8,128)}, f32[512,512]{1,0:T(8,128)})) %all-reduce.3.cloned.1.call-update) | async-done | bytes 2097168 | tf_op jit(solution)/shard_map/psum | solution.py:78
  347.4 2.3 copy.44
  349.6 2.3 copy.45
  (68 shorter events, 21.8 us)
Async XLA Ops:
  7.2 106.0 %copy-start = (bf16[512,512]{1,0:T(8,128)(2,1)S(1)}, bf16[512,512]{1,0:T(8,128)(2,1)}, u32[]{:S(2)}) copy-start(bf16[512,512]{1,0:T(8,128)(2,1)} %param.19) | copy-start | bytes 1572868
  7.2 15.2 %copy-start.1 = (bf16[512,512]{1,0:T(8,128)(2,1)S(1)}, bf16[512,512]{1,0:T(8,128)(2,1)}, u32[]{:S(2)}) copy-start(bf16[512,512]{1,0:T(8,128)(2,1)} %param.13) | copy-start | bytes 1572868
  11.8 33.5 %copy-start.10 = (s32[4,12]{1,0:T(4,128)S(1)}, s32[4,12]{1,0:T(4,128)}, u32[]{:S(2)}) copy-start(s32[4,12]{1,0:T(4,128)} %param.16) | copy-start | bytes 580
  11.8 33.6 %copy-start.9 = (s32[4,12]{1,0:T(4,128)S(1)}, s32[4,12]{1,0:T(4,128)}, u32[]{:S(2)}) copy-start(s32[4,12]{1,0:T(4,128)} %param.17) | copy-start | bytes 580
  11.8 33.6 %copy-start.3 = (bf16[4,12,128,128]{3,2,1,0:T(8,128)(2,1)S(1)}, bf16[4,12,128,128]{3,2,1,0:T(8,128)(2,1)}, u32[]{:S(2)}) copy-start(bf16[4,12,128,128]{3,2,1,0:T(8,128)(2,1)} %param.15) | copy-start | bytes 4718596
  16.0 11.6 %all-to-all-start = ((s32[8,64,1]{1,2,0:T(1,128)}), s32[8,64,1]{1,2,0:T(1,128)S(1)}, u32[]{:S(2)}, u32[]{:S(2)}) async-start(s32[8,64,1]{1,2,0:T(1,128)} %bitcast), calls=%async_computation | async-start | bytes 8192 | tf_op jit(solution)/shard_map/all_to_all | solution.py:58
  22.3 56.4 %copy-start.4 = (bf16[512,512]{1,0:T(8,128)(2,1)S(1)}, bf16[512,512]{1,0:T(8,128)(2,1)}, u32[]{:S(2)}) copy-start(bf16[512,512]{1,0:T(8,128)(2,1)} %param.18) | copy-start | bytes 1572868
  27.6 14.4 %all-to-all-start.1 = ((bf16[8,64,512]{2,1,0:T(8,128)(2,1)}), bf16[8,64,512]{2,1,0:T(8,128)(2,1)S(1)}, u32[]{:S(2)}, u32[]{:S(2)}) async-start(bf16[8,64,512]{2,1,0:T(8,128)(2,1)} %bitcast.2), calls=%async_computation.1 | async-start | bytes 1048576 | tf_op jit(solution)/shard_map/all_to_all | solution.py:57
  31.1 40.1 %all-gather.2.cloned.1.call-start = ((), (), s32[]{:S(2)}) async-start(), calls=%async_computation.3 | async-start | bytes 2621440 | tf_op jit(solution)/shard_map/all_gather | solution.py:65
  45.2 33.5 %copy-start.2 = (bf16[512,512]{1,0:T(8,128)(2,1)S(1)}, bf16[512,512]{1,0:T(8,128)(2,1)}, u32[]{:S(2)}) copy-start(bf16[512,512]{1,0:T(8,128)(2,1)} %scatter_custom_fusion) | copy-start | bytes 1572868
  45.2 162.1 %reduce-scatter.2.cloned.1.call-start = ((), (), s32[]{:S(2)}) async-start(), calls=%async_computation.4 | async-start | bytes 5242880 | tf_op jit(solution)/shard_map/reduce_scatter | solution.py:106
  73.4 25.7 %collective-permute-start = (bf16[512,512]{1,0:T(8,128)(2,1)}, bf16[512,512]{1,0:T(8,128)(2,1)}, u32[]{:S(2)}, u32[]{:S(2)}) collective-permute-start(bf16[512,512]{1,0:T(8,128)(2,1)} %get-tuple-element.39), channel_id=1, source_target_pairs={{0,4},{4,8},{8,12},{12,16},{16,20},{20,24},{24,28},{1,5},{5,9},{9,... | collective-permute-start | bytes 1572872 | tf_op jit(solution)/shard_map/ppermute | solution.py:20
  77.3 21.8 %collective-permute-start.1 = (bf16[512,512]{1,0:T(8,128)(2,1)}, bf16[512,512]{1,0:T(8,128)(2,1)}, u32[]{:S(2)}, u32[]{:S(2)}) collective-permute-start(bf16[512,512]{1,0:T(8,128)(2,1)} %get-tuple-element.40), channel_id=1, source_target_pairs={{4,0},{8,4},{12,8},{16,12},{20,16},{24,20},{28,24},{5,1},{9,5},{13... | collective-permute-start | bytes 1572872 | tf_op jit(solution)/shard_map/ppermute | solution.py:23
  109.1 4.1 %copy-start.6 = (f32[512,512]{1,0:T(8,128)S(1)}, f32[512,512]{1,0:T(8,128)}, u32[]{:S(2)}) copy-start(f32[512,512]{1,0:T(8,128)} %fusion.27) | copy-start | bytes 3145732
  109.1 4.1 %copy-start.11 = (bf16[512,512]{1,0:T(8,128)(2,1)S(1)}, bf16[512,512]{1,0:T(8,128)(2,1)}, u32[]{:S(2)}) copy-start(bf16[512,512]{1,0:T(8,128)(2,1)} %param.21) | copy-start | bytes 1572868
  109.1 4.1 %copy-start.12 = (f32[512]{0:T(512)S(1)}, f32[512]{0:T(512)}, u32[]{:S(2)}) copy-start(f32[512]{0:T(512)} %param.20) | copy-start | bytes 6148
  113.1 2.3 copy-start.7
  130.2 25.4 %collective-permute-start.2 = (bf16[512,512]{1,0:T(8,128)(2,1)S(1)}, bf16[512,512]{1,0:T(8,128)(2,1)S(1)}, u32[]{:S(2)}, u32[]{:S(2)}) collective-permute-start(bf16[512,512]{1,0:T(8,128)(2,1)S(1)} %bitcast.53), channel_id=1, source_target_pairs={{0,4},{4,8},{8,12},{12,16},{16,20},{20,24},{24,28},{1,5},{5,9},{9,... | collective-permute-start | bytes 1572872 | tf_op jit(solution)/shard_map/ppermute | solution.py:12
  134.4 22.4 %collective-permute-start.3 = (bf16[512,512]{1,0:T(8,128)(2,1)S(1)}, bf16[512,512]{1,0:T(8,128)(2,1)S(1)}, u32[]{:S(2)}, u32[]{:S(2)}) collective-permute-start(bf16[512,512]{1,0:T(8,128)(2,1)S(1)} %bitcast.52), channel_id=1, source_target_pairs={{4,0},{8,4},{12,8},{16,12},{20,16},{24,20},{28,24},{5,1},{9,5},{13... | collective-permute-start | bytes 1572872 | tf_op jit(solution)/shard_map/ppermute | solution.py:12
  155.6 3.6 %copy-start.8 = (bf16[4,128,512]{2,1,0:T(8,128)(2,1)S(1)}, bf16[4,128,512]{2,1,0:T(8,128)(2,1)}, u32[]{:S(2)}) copy-start(bf16[4,128,512]{2,1,0:T(8,128)(2,1)} %copy-done.7) | copy-start | bytes 1572868
  159.2 46.3 %copy-start.5 = (bf16[512,512]{1,0:T(8,128)(2,1)S(1)}, bf16[512,512]{1,0:T(8,128)(2,1)}, u32[]{:S(2)}) copy-start(bf16[512,512]{1,0:T(8,128)(2,1)} %param.18) | copy-start | bytes 1572868
  159.2 188.2 %all-reduce.3.cloned.1.call-start = ((), (), s32[]{:S(2)}) async-start(), calls=%async_computation.5 | async-start | bytes 4194304 | tf_op jit(solution)/shard_map/psum | solution.py:78
Sparse Core Ops, SparseCore 0:
  45.3 25.8 all-gather.1
  159.3 47.9 reduce-scatter.1
  214.3 133.0 all-reduce.2
where the time goes:
time: 361 us; the launch traced here: 358 us
  waiting for transfers between devices  210 us (58%)
  blocking collectives  43.4 us (12%)
  local copies, waits for them, and re-layouts  31 us (9%)
  matrix products  25.2 us (7%)
  starting transfers between devices  20.6 us (6%)
  other arithmetic  14.6 us (4%)
  between operations  14 us (4%)
    psum x1, waiting for transfers between devices, shards(): lax.psum((contract_rows(features, dz), contract_rows(agg, dz), jnp.sum(dz...  138 us
    psum x1, blocking collectives, shards(): lax.psum((contract_rows(features, dz), contract_rows(agg, dz), jnp.sum(dz...  43.4 us
    all_gather x1, waiting for transfers between devices, shards(): whole = lax.all_gather(features, 'rep', axis=0, tiled=True)  25.4 us
    ppermute x1, waiting for transfers between devices, with_halo(): lax.ppermute(lax.slice_in_dim(block, block.shape[dim] - width, None, axis...  19 us
    ppermute x2, waiting for transfers between devices, shifted(): lax.ppermute(value, axis, [(source, source + steps) for source in range(f...  13.9 us
    dot_general x1, matrix products, shards(): jnp.einsum('en,nbf->ebf', selector, terms.reshape(-1, 128, width), precis...  12.3 us
    all_to_all x1, waiting for transfers between devices, shards(): lax.all_to_all(x_loader[order], 'dom', split_axis=0, concat_axis=0, tiled...  9.61 us
  transfers between devices with their start and end apart: 9, of which 7 were waited for; matrix products, arithmetic and copies ran while one was open for 5% of the time, Pallas kernels for 0%

commit v1 on v0

v1 whole, which is shorter than its diff:
```python
import functools

import jax
import jax.numpy as jnp
from jax import lax
from jax.experimental import pallas as pl
from jax.experimental.pallas import tpu as pltpu
from jax.sharding import PartitionSpec as P

HALO_T = 4
LANES = 128
PIECES = 2
MESH = pl.DeviceIdType.MESH
F32 = jnp.float32
BF16 = jnp.bfloat16


def dot(a, b):
    return jnp.dot(a, b, preferred_element_type=F32)


def dot_rows(a, b):
    return lax.dot_general(a, b, (((0,), (0,)), ((), ())), preferred_element_type=F32)


def dot_cols(a, b):
    return lax.dot_general(a, b, (((1,), (1,)), ((), ())), preferred_element_type=F32)


def kernel(
    parts, reps,
    x_ref, owner_ref, vals_ref, cols_ref, live_ref, ws_ref, wn_ref, bias_ref, cot_ref,
    out_ref, gf_ref, gs_ref, gn_ref, gb_ref,
    mv_send, mv_recv, sl_send, sl_recv, fa, ext_f, ext_s, wm, deg, dz, brow,
    a_send, a_recv, b_send, b_recv, fin, bias_a, bias_b,
    mv_ss, mv_rs, sl_ss, sl_rs, e_ss, e_rs,
    a_ss, a_rs, b_ss, b_rs, gb_ss, gb_rs, ga_ss, ga_rs, ba_ss, ba_rs, bb_ss, bb_rs,
):
    p = lax.axis_index("dom")
    r = lax.axis_index("rep")
    rows, width = x_ref.shape
    tiles = rows // LANES
    slots = vals_ref.shape[1]
    share = rows // parts
    piece = tiles // PIECES
    r1 = r + 1 - 2 * lax.rem(r, 2)
    r2 = lax.rem(r + 2, 4)
    r3 = 3 - r

    def remote(src, dst, ss, rs, dom, rep):
        return pltpu.make_async_remote_copy(
            src_ref=src, dst_ref=dst, send_sem=ss, recv_sem=rs,
            device_id=(dom, rep), device_id_type=MESH,
        )

    barrier = pltpu.get_barrier_semaphore()
    for i in range(1, reps):
        pl.semaphore_signal(barrier, inc=1, device_id=(p, lax.rem(r + i, reps)), device_id_type=MESH)
    for i in range(1, parts):
        pl.semaphore_signal(barrier, inc=1, device_id=(lax.rem(p + i, parts), r), device_id_type=MESH)

    owner = owner_ref[...]
    dest = lax.div(owner, rows * reps)
    slot = lax.rem(owner, rows)
    kinds = max(parts, 16)
    hot = lax.broadcasted_iota(jnp.int32, (kinds, rows), 0) == dest
    before = (
        lax.broadcasted_iota(jnp.int32, (rows, rows), 0)
        < lax.broadcasted_iota(jnp.int32, (rows, rows), 1)
    ).astype(F32).astype(BF16)
    counts = dot(hot.astype(F32).astype(BF16), before)
    rank = jnp.sum(jnp.where(hot, counts, 0.0), axis=0, keepdims=True)
    pos = dest * share + rank.astype(jnp.int32)
    pick = lax.broadcasted_iota(jnp.int32, (rows, rows), 0) == pos
    moved = dot(pick.astype(F32).astype(BF16), x_ref[...]).astype(BF16)
    where_to = jnp.sum(jnp.where(pick, slot.astype(F32), 0.0), axis=1, keepdims=True)
    mv_send[...] = moved.reshape(parts, share, width)
    sl_send[...] = jnp.broadcast_to(where_to.astype(jnp.int32), (rows, LANES)).reshape(parts, share, LANES)

    pl.semaphore_wait(barrier, reps - 1 + parts - 1)

    def to_parts(src, dst, ss, rs, i):
        peer = lax.rem(p + i, parts)
        return remote(src(peer), dst(p), ss.at[i], rs.at[p], peer, r)

    def from_parts(src, dst, ss, rs, i):
        peer = lax.rem(p + parts - i, parts)
        return remote(src(peer), dst(peer), ss.at[i], rs.at[peer], peer, r)

    def to_reps(src, dst, ss, rs, i):
        peer = lax.rem(r + i, reps)
        return remote(src(peer), dst(r), ss.at[i], rs.at[r], p, peer)

    def from_reps(src, dst, ss, rs, i):
        peer = lax.rem(r + reps - i, reps)
        return remote(src(peer), dst(peer), ss.at[i], rs.at[peer], p, peer)

    def at(ref):
        return lambda k: ref.at[k]

    sl = (at(sl_send), at(sl_recv), sl_ss, sl_rs)
    mv = (at(mv_send), at(mv_recv), mv_ss, mv_rs)
    for i in range(1, parts):
        to_parts(*mv, i).start()
        to_parts(*sl, i).start()
    mv_recv[p] = mv_send[p]
    sl_recv[p] = sl_send[p]

    def mask_tiles(t, carry):
        total = jnp.zeros((LANES, LANES), F32)
        for k in range(slots):
            tile = vals_ref[t, k].astype(F32) * live_ref[t, k].astype(F32)
            total = total + tile
            wm[t, :, k * LANES:(k + 1) * LANES] = tile.astype(BF16)
        degree = 1.0 + jnp.sum(total, axis=1, keepdims=True)
        deg[t] = jnp.broadcast_to(degree, (LANES, LANES))
        return carry

    lax.fori_loop(0, tiles, mask_tiles, 0)

    for i in range(1, parts):
        from_parts(*mv, i).wait_recv()
        from_parts(*sl, i).wait_recv()
    landed = sl_recv[...].reshape(rows, LANES)
    place = jnp.concatenate(
        [
            (landed == lax.broadcasted_iota(jnp.int32, (rows, LANES), 1) + c * LANES).astype(F32).astype(BF16)
            for c in range(rows // LANES)
        ],
        axis=1,
    )
    features = dot_rows(place, mv_recv[...].reshape(rows, width)).astype(BF16)
    fa[0] = features
    first = HALO_T + r * tiles
    ext_f[pl.ds(first, tiles)] = features.reshape(tiles, LANES, width)

    def spread(ext, use):
        high = HALO_T + reps * tiles

        def copy(base, c, send, recv, dom, rep, target=None):
            src = ext.at[pl.ds(base + c * piece, piece)]
            dst = src if target is None else ext.at[pl.ds(target + c * piece, piece)]
            return remote(src, dst, e_ss.at[use, send, c], e_rs.at[use, recv, c], dom, rep)

        def block(q):
            return HALO_T + q * tiles

        root_low, root_high = r == reps - 1, r == 0
        more, less = p < parts - 1, p > 0

        def begin():
            for c in range(PIECES):
                copy(block(r), c, 0, 0, p, r2).start()

                @pl.when(jnp.logical_and(root_low, more))
                def _():
                    copy(block(r), c, 3, 3, p + 1, r, 0).start()

                @pl.when(jnp.logical_and(root_high, less))
                def _():
                    copy(block(r), c, 4, 4, p - 1, r, high).start()

                copy(block(r), c, 1, 1, p, r1).start()

        def rim(base, c, recv, send, root, second, there):
            @pl.when(there)
            def _():
                copy(base, c, send, recv, p, r1).wait_recv()

                @pl.when(root)
                def _():
                    copy(base, c, send + 1, recv, p, r2).start()
                    copy(base, c, send, recv, p, r1).start()

                @pl.when(second)
                def _():
                    copy(base, c, send, recv, p, r1).start()

        def forward():
            for c in range(PIECES):
                copy(block(r2), c, 0, 0, p, r2).wait_recv()
                copy(block(r2), c, 2, 2, p, r1).start()
                rim(0, c, 3, 5, root_low, r == 1, less)
                rim(high, c, 4, 7, root_high, r == 2, more)

        def end():
            for c in range(PIECES):
                copy(block(r1), c, 1, 1, p, r1).wait_recv()
                copy(block(r3), c, 2, 2, p, r1).wait_recv()

        def sent():
            for c in range(PIECES):
                copy(block(r), c, 0, 0, p, r2).wait_send()
                copy(block(r), c, 1, 1, p, r1).wait_send()
                copy(block(r2), c, 2, 2, p, r1).wait_send()

                @pl.when(jnp.logical_and(root_low, more))
                def _():
                    copy(block(r), c, 3, 3, p + 1, r, 0).wait_send()

                @pl.when(jnp.logical_and(root_high, less))
                def _():
                    copy(block(r), c, 4, 4, p - 1, r, high).wait_send()

                for base, recv, send, root, second, there in (
                    (0, 3, 5, root_low, r == 1, less),
                    (high, 4, 7, root_high, r == 2, more),
                ):
                    @pl.when(jnp.logical_and(there, root))
                    def _():
                        copy(base, c, send + 1, recv, p, r2).wait_send()
                        copy(base, c, send, recv, p, r1).wait_send()

                    @pl.when(jnp.logical_and(there, second))
                    def _():
                        copy(base, c, send, recv, p, r1).wait_send()

        return begin, forward, end, sent

    begin_f, forward_f, end_f, sent_f = spread(ext_f, 0)
    begin_s, forward_s, end_s, sent_s = spread(ext_s, 1)
    first_tile = p * (reps * tiles) - HALO_T

    def gather(ext, t):
        last = ext.shape[0] - 1
        picked = [ext[jnp.clip(cols_ref[t, k] - first_tile, 0, last)] for k in range(slots)]
        return jnp.concatenate(picked, axis=0)

    begin_f()
    forward_f()
    end_f()

    brow[...] = jnp.zeros(brow.shape, F32)

    def layer(t, carry):
        here = pl.ds(pl.multiple_of(t * LANES, LANES), LANES)
        degree = deg[t][:, 0:1]
        agg = (dot(wm[t], gather(ext_f, t)) / degree).astype(BF16)
        fa[1, here] = agg
        pre = dot(fa[0, here], ws_ref[...]) + dot(agg, wn_ref[...]) + bias_ref[...]
        decay = jnp.exp(jnp.minimum(pre, 0.0))
        out_ref[here] = jnp.where(pre > 0, pre, decay - 1.0).astype(BF16)
        slope = jnp.where(pre > 0, 1.0, decay)
        grad = (cot_ref[here].astype(F32) * slope).astype(BF16)
        dz[here] = grad
        brow[...] += jnp.broadcast_to(jnp.sum(grad.astype(F32), axis=0, keepdims=True), brow.shape)
        ext_s[first + t] = (dot_cols(grad, wn_ref[...]) / degree).astype(BF16)
        return carry

    lax.fori_loop(0, tiles, layer, 0)
    begin_s()

    quarter = 2 * width // reps
    per = reps // 2

    def weight(q, carry):
        column = pl.multiple_of(lax.rem(q, per) * quarter, quarter)
        a_send[q] = dot_rows(fa[lax.div(q, per), :, pl.ds(column, quarter)], dz[...]).astype(BF16)
        return carry

    lax.fori_loop(0, reps, weight, 0)
    bias_a[r] = brow[...]
    a = (at(a_send), at(a_recv), a_ss, a_rs)
    ba = (lambda k: bias_a.at[r], at(bias_a), ba_ss, ba_rs)
    for i in range(1, reps):
        to_reps(*a, i).start()
        to_reps(*ba, i).start()
    a_recv[r] = a_send[r]
    forward_s()

    for i in range(1, reps):
        from_reps(*a, i).wait_recv()
        from_reps(*ba, i).wait_recv()
    high_c, wide_c = b_send.shape[1:]
    across = width // wide_c
    for d in range(parts):
        down, side = d // across * high_c, d % across * wide_c
        total = jnp.zeros((high_c, wide_c), F32)
        for q in range(reps):
            total = total + a_recv[q, down:down + high_c, side:side + wide_c].astype(F32)
        b_send[d] = total.astype(BF16)
    total = bias_a[0]
    for q in range(1, reps):
        total = total + bias_a[q]
    bias_b[p] = total
    b = (at(b_send), at(b_recv), b_ss, b_rs)
    bb = (lambda k: bias_b.at[p], at(bias_b), bb_ss, bb_rs)
    for i in range(1, parts):
        to_parts(*b, i).start()
        to_parts(*bb, i).start()
    b_recv[p] = b_send[p]
    end_s()

    for i in range(1, parts):
        from_parts(*b, i).wait_recv()
        from_parts(*bb, i).wait_recv()
    total = b_recv[0].astype(F32)
    bias_total = bias_b[0]
    for d in range(1, parts):
        total = total + b_recv[d].astype(F32)
        bias_total = bias_total + bias_b[d]
    fin[r, p] = total.astype(BF16)
    gb_ref[...] = bias_total[0:1]
    gb = (lambda k: fin.at[r, p], lambda k: fin.at[r, k], gb_ss, gb_rs)
    for i in range(1, parts):
        to_parts(*gb, i).start()

    def back(t, carry):
        here = pl.ds(pl.multiple_of(t * LANES, LANES), LANES)
        gf_ref[here] = (
            dot_cols(dz[here], ws_ref[...]) + dot(wm[t], gather(ext_s, t))
        ).astype(BF16)
        return carry

    lax.fori_loop(0, tiles, back, 0)

    for i in range(1, parts):
        from_parts(*gb, i).wait_recv()
    ga = (lambda k: fin.at[r], at(fin), ga_ss, ga_rs)
    for i in range(1, reps):
        to_reps(*ga, i).start()
    for i in range(1, reps):
        from_reps(*ga, i).wait_recv()
    for q in range(reps):
        ref = gs_ref if q < per else gn_ref
        for d in range(parts):
            down, side = q % per * quarter + d // across * high_c, d % across * wide_c
            ref[down:down + high_c, side:side + wide_c] = fin[q, d].astype(F32)

    for i in range(1, parts):
        for kind in (mv, sl, b, bb, gb):
            to_parts(*kind, i).wait_send()
    for i in range(1, reps):
        for kind in (a, ba, ga):
            to_reps(*kind, i).wait_send()
    sent_f()
    sent_s()


def shards(
    parts, reps,
    x_loader, owner_index, tile_vals, tile_cols, tile_live, w_self, w_neigh, bias, cotangent
):
    rows, width = x_loader.shape
    tiles, slots = tile_cols.shape
    share = rows // parts
    quarter = 2 * width // reps
    high_c = max(16, quarter // parts)
    wide_c = quarter * width // parts // high_c
    span = reps * tiles + 2 * HALO_T
    dma = pltpu.SemaphoreType.DMA
    vmem = pl.BlockSpec(memory_space=pltpu.VMEM)
    smem = pl.BlockSpec(memory_space=pltpu.SMEM)
    out = pl.pallas_call(
        functools.partial(kernel, parts, reps),
        out_shape=(
            jax.ShapeDtypeStruct((rows, width), BF16),
            jax.ShapeDtypeStruct((rows, width), BF16),
            jax.ShapeDtypeStruct((width, width), F32),
            jax.ShapeDtypeStruct((width, width), F32),
            jax.ShapeDtypeStruct((1, width), F32),
        ),
        in_specs=[vmem, vmem, vmem, smem, smem, vmem, vmem, vmem, vmem],
        out_specs=(vmem,) * 5,
        scratch_shapes=[
            pltpu.VMEM((parts, share, width), BF16),
            pltpu.VMEM((parts, share, width), BF16),
            pltpu.VMEM((parts, share, LANES), jnp.int32),
            pltpu.VMEM((parts, share, LANES), jnp.int32),
            pltpu.VMEM((2, rows, width), BF16),
            pltpu.VMEM((span, LANES, width), BF16),
            pltpu.VMEM((span, LANES, width), BF16),
            pltpu.VMEM((tiles, LANES, slots * LANES), BF16),
            pltpu.VMEM((tiles, LANES, LANES), F32),
            pltpu.VMEM((rows, width), BF16),
            pltpu.VMEM((8, width), F32),
            pltpu.VMEM((reps, quarter, width), BF16),
            pltpu.VMEM((reps, quarter, width), BF16),
            pltpu.VMEM((parts, high_c, wide_c), BF16),
            pltpu.VMEM((parts, high_c, wide_c), BF16),
            pltpu.VMEM((reps, parts, high_c, wide_c), BF16),
            pltpu.VMEM((reps, 8, width), F32),
            pltpu.VMEM((parts, 8, width), F32),
            dma((parts,)), dma((parts,)), dma((parts,)), dma((parts,)),
            dma((2, 9, PIECES)), dma((2, 5, PIECES)),
            dma((reps,)), dma((reps,)), dma((parts,)), dma((parts,)),
            dma((parts,)), dma((parts,)), dma((reps,)), dma((reps,)),
            dma((reps,)), dma((reps,)), dma((parts,)), dma((parts,)),
        ],
        compiler_params=pltpu.CompilerParams(
            collective_id=0, has_side_effects=True, vmem_limit_bytes=48 * 1024 * 1024
        ),
    )(
        x_loader, owner_index.reshape(1, rows), tile_vals, tile_cols, tile_live,
        w_self, w_neigh, bias.reshape(1, width), cotangent,
    )
    return (*out[:4], out[4].reshape(width))


def solution(mesh):
    sharded = P(("dom", "rep"))
    return jax.shard_map(
        functools.partial(shards, mesh.shape["dom"], mesh.shape["rep"]),
        mesh=mesh,
        in_specs=(sharded,) * 5 + (P(), P(), P(), sharded),
        out_specs=(sharded, sharded, P(), P(), P()),
        check_vma=False,
    )
```

time: 361 us -> 154 us (0.43)
  waiting for transfers between devices: 210 us -> 0 us
  Pallas kernels: 0 us -> 142 us
  blocking collectives: 43.4 us -> 0 us
  matrix products: 25.2 us -> 0 us
  starting transfers between devices: 20.6 us -> 0 us
  local copies, waits for them, and re-layouts: 31 us -> 11 us
  other arithmetic: 14.6 us -> 0 us
  between operations: 14 us -> 0.66 us
    pallas_call x0 -> x1, Pallas kernels: none -> 142 us  [shards(): pl.pallas_call(functools.partial(kernel, parts, reps), out_shape=(jax.Sha...]
    psum x1 -> x0, waiting for transfers between devices: 138 us -> none  [shards(): lax.psum((contract_rows(features, dz), contract_rows(agg, dz), jnp.sum(dz...]
    psum x1 -> x0, blocking collectives: 43.4 us -> none  [shards(): lax.psum((contract_rows(features, dz), contract_rows(agg, dz), jnp.sum(dz...]
    ppermute x4 -> x0, waiting for transfers between devices: 32.8 us -> none  [the longest x1 19 us: with_halo(): lax.ppermute(lax.slice_in_dim(block, block.shape[dim] - width, None, axis...]
    all_gather x1 -> x0, waiting for transfers between devices: 25.4 us -> none  [shards(): whole = lax.all_gather(features, 'rep', axis=0, tiled=True)]
    dot_general x9 -> x0, matrix products: 25.2 us -> none  [the longest x1 12.3 us: shards(): jnp.einsum('en,nbf->ebf', selector, terms.reshape(-1, 128, width), precis...]
    gather x3 -> x0, local copies, waits for them, and re-layouts: 13 us -> none  [the longest x1 6.86 us: shards(): picked = extended.reshape(-1, 128, width)[local_cols]]
    all_to_all x2 -> x0, waiting for transfers between devices: 12.2 us -> none  [the longest x1 9.61 us: shards(): lax.all_to_all(x_loader[order], 'dom', split_axis=0, concat_axis=0, tiled...]
  transfers between devices with their start and end apart: 9 -> 0, of which waited for: 7 -> 0; matrix products, arithmetic and copies ran while one was open for 5% -> 0% of each run, Pallas kernels for 0% -> 0%
where the time goes in v1:
time: 154 us
  Pallas kernels  142 us (92%)
  local copies, waits for them, and re-layouts  11 us (7%)
    pallas_call x1, Pallas kernels, shards(): pl.pallas_call(functools.partial(kernel, parts, reps), out_shape=(jax.Sha...  142 us
    unnamed x21, local copies, waits for them, and re-layouts  11 us

profile of v1, /device:TPU:1, one launch (start us, length us, event | category | flops | bytes accessed | tf_op | source)
XLA Modules:
  0.0 154.0 jit_solution(8395404586989359233)
XLA Ops:
  0.6 0.0 copy-start
  0.6 1.0 copy-done
  1.7 0.0 copy-start.1
  1.7 1.0 copy-done.1
  2.7 0.0 copy-start.2
  2.7 1.0 copy-done.2
  3.8 0.0 copy-start.3
  3.8 1.0 copy-done.3
  4.8 0.0 copy-start.4
  4.8 0.7 copy-done.4
  5.5 0.0 copy-start.5
  5.5 0.7 copy-done.5
  6.2 0.0 copy-start.6
  6.2 0.7 copy-done.6
  6.8 0.0 copy-start.7
  6.9 0.7 copy-done.7
  7.5 142.3 %shard_map.128 = (bf16[512,512]{1,0:T(8,128)(2,1)S(1)}, bf16[512,512]{1,0:T(8,128)(2,1)S(1)}, f32[512,512]{1,0:T(8,128)S(1)}, f32[512,512]{1,0:T(8,128)S(1)}, f32[1,512]{1,0:T(1,128)S(1)}) custom-call(bf16[512,512]{1,0:T(8,128)(2,1)S(1)} %copy-done, s32[1,512]{1,0:T(1,128)S(1)} %bitcast.3, bf16[4,12,128,128]{3,2,1,0:T(8,128)(2,1)} %vals_ref.1, ...), custom_call_target="tpu_custom_call" | custom-call | tf_op jit(solution)/shard_map/pallas_call | solution.py:354
  149.9 0.8 copy.19
  150.7 0.8 copy.20
  151.5 1.0 copy.21
  152.4 1.0 copy.22
  153.4 0.6 copy.23
Async XLA Ops:
  0.6 1.0 copy-start
  1.7 1.0 copy-start.1
  2.7 1.0 copy-start.2
  3.8 1.0 copy-start.3
  4.8 0.7 copy-start.4
  5.5 0.7 copy-start.5
  6.2 0.7 copy-start.6
  6.8 0.7 copy-start.7

commit v2 on v1

--- a/solution.py
+++ b/solution.py
@@ -260,23 +260,33 @@
 
     lax.fori_loop(0, reps, weight, 0)
     bias_a[r] = brow[...]
-    a = (at(a_send), at(a_recv), a_ss, a_rs)
+
+    def a_copy(src, k, peer):
+        return remote(src, a_recv.at[k], a_ss.at[k], a_rs.at[k], p, peer)
+
+    cross = a_copy(a_send.at[r3], 1, r1)
+    near = a_copy(a_send.at[r1], 0, r1)
+    far = a_copy(a_recv.at[3], 2, r2)
+    cross.start()
+    near.start()
     ba = (lambda k: bias_a.at[r], at(bias_a), ba_ss, ba_rs)
     for i in range(1, reps):
-        to_reps(*a, i).start()
         to_reps(*ba, i).start()
-    a_recv[r] = a_send[r]
+    cross.wait_recv()
+    a_recv[3] = (a_send[r2].astype(F32) + a_recv[1].astype(F32)).astype(BF16)
+    far.start()
     forward_s()
 
     for i in range(1, reps):
-        from_reps(*a, i).wait_recv()
         from_reps(*ba, i).wait_recv()
+    near.wait_recv()
+    far.wait_recv()
     high_c, wide_c = b_send.shape[1:]
     across = width // wide_c
     for d in range(parts):
         down, side = d // across * high_c, d % across * wide_c
-        total = jnp.zeros((high_c, wide_c), F32)
-        for q in range(reps):
+        total = a_send[r, down:down + high_c, side:side + wide_c].astype(F32)
+        for q in (0, 2):
             total = total + a_recv[q, down:down + high_c, side:side + wide_c].astype(F32)
         b_send[d] = total.astype(BF16)
     total = bias_a[0]
@@ -316,11 +326,16 @@
 
     for i in range(1, parts):
         from_parts(*gb, i).wait_recv()
-    ga = (lambda k: fin.at[r], at(fin), ga_ss, ga_rs)
-    for i in range(1, reps):
-        to_reps(*ga, i).start()
-    for i in range(1, reps):
-        from_reps(*ga, i).wait_recv()
+
+    def g_copy(k, send, peer):
+        return remote(fin.at[k], fin.at[k], ga_ss.at[send], ga_rs.at[k], p, peer)
+
+    g_copy(r, 0, r2).start()
+    g_copy(r, 1, r1).start()
+    g_copy(r2, 0, r2).wait_recv()
+    g_copy(r2, 2, r1).start()
+    g_copy(r1, 1, r1).wait_recv()
+    g_copy(r3, 2, r1).wait_recv()
     for q in range(reps):
         ref = gs_ref if q < per else gn_ref
         for d in range(parts):
@@ -331,8 +346,9 @@
         for kind in (mv, sl, b, bb, gb):
             to_parts(*kind, i).wait_send()
     for i in range(1, reps):
-        for kind in (a, ba, ga):
-            to_reps(*kind, i).wait_send()
+        to_reps(*ba, i).wait_send()
+    for copy in (cross, near, far, g_copy(r, 0, r2), g_copy(r, 1, r1), g_copy(r2, 2, r1)):
+        copy.wait_send()
     sent_f()
     sent_s()
 

time: 154 us -> 145 us (0.942)
  Pallas kernels: 142 us -> 133 us
    pallas_call x1, Pallas kernels: 142 us -> 133 us  [shards(): pl.pallas_call(functools.partial(kernel, parts, reps), out_shape=(jax.Sha...]
where the time goes in v2:
time: 145 us; the launch traced here: 144 us
  Pallas kernels  133 us (92%)
  local copies, waits for them, and re-layouts  11 us (8%)
    pallas_call x1, Pallas kernels, shards(): pl.pallas_call(functools.partial(kernel, parts, reps), out_shape=(jax.Sha...  133 us
    unnamed x21, local copies, waits for them, and re-layouts  11 us

profile of v2, /device:TPU:1, one launch (start us, length us, event | category | flops | bytes accessed | tf_op | source)
XLA Modules:
  0.0 144.4 jit_solution(14945079002819119389)
XLA Ops:
  0.6 0.0 copy-start
  0.6 1.0 copy-done
  1.7 0.0 copy-start.1
  1.7 1.0 copy-done.1
  2.7 0.0 copy-start.2
  2.7 1.0 copy-done.2
  3.8 0.0 copy-start.3
  3.8 1.0 copy-done.3
  4.8 0.0 copy-start.4
  4.8 0.7 copy-done.4
  5.5 0.0 copy-start.5
  5.5 0.7 copy-done.5
  6.2 0.0 copy-start.6
  6.2 0.7 copy-done.6
  6.8 0.0 copy-start.7
  6.9 0.7 copy-done.7
  7.5 132.8 %shard_map.128 = (bf16[512,512]{1,0:T(8,128)(2,1)S(1)}, bf16[512,512]{1,0:T(8,128)(2,1)S(1)}, f32[512,512]{1,0:T(8,128)S(1)}, f32[512,512]{1,0:T(8,128)S(1)}, f32[1,512]{1,0:T(1,128)S(1)}) custom-call(bf16[512,512]{1,0:T(8,128)(2,1)S(1)} %copy-done, s32[1,512]{1,0:T(1,128)S(1)} %bitcast.3, bf16[4,12,128,128]{3,2,1,0:T(8,128)(2,1)} %vals_ref.1, ...), custom_call_target="tpu_custom_call" | custom-call | tf_op jit(solution)/shard_map/pallas_call | solution.py:370
  140.3 0.8 copy.19
  141.1 0.8 copy.20
  141.9 1.0 copy.21
  142.9 1.0 copy.22
  143.8 0.6 copy.23
Async XLA Ops:
  0.6 1.0 copy-start
  1.7 1.0 copy-start.1
  2.7 1.0 copy-start.2
  3.8 1.0 copy-start.3
  4.8 0.7 copy-start.4
  5.5 0.7 copy-start.5
  6.2 0.7 copy-start.6
  6.8 0.7 copy-start.7
